TPU v7x, 512 devices: a whole 4x8x8 slice. The times are simulated.
512 devices in a mesh: dp: 32 (over z, y_hi), fsdp: 16 (over x, y_lo, core).
Axes of the slice: x: 4, y: 8 (y_hi: 4, y_lo: 2; y = y_hi * 2 + y_lo), z: 8, core: 2. Of those that a mesh axis runs over, the one named last changes fastest.
Arguments:
- tokens: bfloat16 [12288, 4096], P('dp', 'fsdp'), may hold values from -6 to 6
- gate_logits: bfloat16 [12288, 14336], P('dp', 'fsdp'), may hold values from -8 to 8
- linear_values: bfloat16 [12288, 14336], P('dp', 'fsdp'), may hold values from -6 to 6
- hidden_grad: bfloat16 [12288, 14336], P('dp', 'fsdp'), may hold values from -3 to 3
- basis: bfloat16 [4096, 512], P('fsdp'), may hold values from -0.09375 to 0.09375
- gate_moment: float32 [512, 14336], P('dp', 'fsdp'), may hold values from -0.75 to 0.75
- gate_second: float32 [512, 14336], P('dp', 'fsdp'), may hold values from 0.05 to 1
- linear_moment: float32 [512, 14336], P('dp', 'fsdp'), may hold values from -0.75 to 0.75
- linear_second: float32 [512, 14336], P('dp', 'fsdp'), may hold values from 0.05 to 1
Outputs:
- gate_update: float32 [4096, 14336], P('dp', 'fsdp')
- linear_update: float32 [4096, 14336], P('dp', 'fsdp')
- moment_gate: float32 [512, 14336], P('dp', 'fsdp')
- second_gate: float32 [512, 14336], P('dp', 'fsdp')
- moment_linear: float32 [512, 14336], P('dp', 'fsdp')
- second_linear: float32 [512, 14336], P('dp', 'fsdp')
All inputs are finite; a program needn't handle non-finite values.
Results may differ from a plain program's by a relative error of at most 0.0057.
Values may be sent and summed in bfloat16 or wider, within the bound.
A program may use at most 64 MiB of HBM per device.

v0:
```python
import jax
import jax.numpy as jnp
from jax import lax
from jax.sharding import PartitionSpec as P


def spread(value, axis, source):
    kept = jnp.where(lax.axis_index(axis) == source, value, 0).astype(value.dtype)
    return lax.psum(kept, axis)


def gradients(gate_logits, linear_values, hidden_grad):
    logits = gate_logits.astype(jnp.float32)
    values = linear_values.astype(jnp.float32)
    incoming = hidden_grad.astype(jnp.float32)
    sigmoid_gate = jax.nn.sigmoid(logits)
    activated = logits * sigmoid_gate
    gate_grad = (incoming * values * sigmoid_gate * (1.0 + logits * (1.0 - sigmoid_gate))).astype(
        jnp.bfloat16
    )
    linear_grad = (incoming * activated).astype(jnp.bfloat16)
    return (gate_grad, linear_grad)


def adam_step(moment, second, grad):
    moment_out = 0.9 * moment + 0.1 * grad
    second_out = 0.999 * second + 0.001 * grad * grad
    normalized = (moment_out / (jnp.sqrt(second_out) + 1e-08)).astype(jnp.bfloat16)
    return (moment_out, second_out, normalized)


def per_device(
    tokens,
    gate_logits,
    linear_values,
    hidden_grad,
    basis,
    gate_moment,
    gate_second,
    linear_moment,
    linear_second,
):
    block_rows = basis.shape[0]
    width = gate_logits.shape[1]
    rows_dp = block_rows * lax.axis_size("fsdp") // lax.axis_size("dp")
    features = lax.all_gather(tokens, "fsdp", axis=1, tiled=True)
    summed_proj = jnp.dot(
        features,
        lax.all_gather(basis, "fsdp", axis=0, tiled=True),
        preferred_element_type=jnp.float32,
    )
    projected = summed_proj.astype(jnp.bfloat16)
    gate_grad, linear_grad = gradients(gate_logits, linear_values, hidden_grad)
    first_row = lax.axis_index("dp") * rows_dp
    holder = first_row // block_rows
    block = spread(basis, "fsdp", holder)
    local_rows = lax.dynamic_slice_in_dim(block, first_row % block_rows, rows_dp, 0)

    def expand_one(piece):
        return jnp.dot(local_rows, piece, preferred_element_type=jnp.float32)

    both = jnp.concatenate([gate_grad, linear_grad], axis=1)
    subspace = lax.psum_scatter(
        lax.dot_general(
            projected, both, (((0,), (0,)), ((), ())), preferred_element_type=jnp.float32
        ),
        "dp",
        scatter_dimension=0,
        tiled=True,
    )
    moment_gate, second_gate, gate_norm = adam_step(gate_moment, gate_second, subspace[:, :width])
    moment_linear, second_linear, linear_norm = adam_step(
        linear_moment, linear_second, subspace[:, width:]
    )
    gate_update = expand_one(lax.all_gather(gate_norm, "dp", axis=0, tiled=True))
    linear_update = expand_one(lax.all_gather(linear_norm, "dp", axis=0, tiled=True))
    return (gate_update, linear_update, moment_gate, second_gate, moment_linear, second_linear)


def solution(mesh):
    placed = (
        P("dp", "fsdp"),
        P("dp", "fsdp"),
        P("dp", "fsdp"),
        P("dp", "fsdp"),
        P("fsdp", None),
        P("dp", "fsdp"),
        P("dp", "fsdp"),
        P("dp", "fsdp"),
        P("dp", "fsdp"),
    )
    return jax.shard_map(
        per_device,
        mesh=mesh,
        in_specs=placed,
        out_specs=(
            P("dp", "fsdp"),
            P("dp", "fsdp"),
            P("dp", "fsdp"),
            P("dp", "fsdp"),
            P("dp", "fsdp"),
            P("dp", "fsdp"),
        ),
        check_vma=False,
    )
```

profile of v0, /device:TPU:16, one launch (start us, length us, event | category | flops | bytes accessed | tf_op | source)
XLA Modules:
  0.0 524.1 jit_solution(9659957795164064031)
XLA Ops:
  7.2 0.0 all-gather.3.cloned.1.call-start
  7.2 0.7 all-gather.3.cloned.1.call-update
  7.9 0.0 all-gather.5.cloned.1.call-start
  7.9 0.7 all-gather.5.cloned.1.call-update
  8.7 0.0 reduce-scatter.2.cloned.1.call-start
  8.7 2.3 fusion.2
  11.0 50.0 %all-gather.3.cloned.1.call-done = bf16[384,4096]{1,0:T(8,128)(2,1)} async-done(((bf16[384,256]{1,0:T(8,128)(2,1)}), bf16[384,4096]{1,0:T(8,128)(2,1)}) %all-gather.3.cloned.1.call-update) | async-done | bytes 3145744 | tf_op jit(solution)/shard_map/all_gather | solution.py:46
  61.0 45.0 %all-gather.5.cloned.1.call-done = bf16[4096,512]{1,0:T(8,128)(2,1)} async-done(((bf16[256,512]{1,0:T(8,128)(2,1)}), bf16[4096,512]{1,0:T(8,128)(2,1)}) %all-gather.5.cloned.1.call-update) | async-done | bytes 4194320 | tf_op jit(solution)/shard_map/all_gather | solution.py:49
  106.0 7.8 %fusion.8 = f32[512,1792]{1,0:T(8,128)} fusion(bf16[384,896]{1,0:T(8,128)(2,1)S(1)} %get-tuple-element.13, bf16[384,896]{1,0:T(8,128)(2,1)S(1)} %get-tuple-element.12, bf16[384,4096]{1,0:T(8,128)(2,1)} %all-gather.3.cloned.1.call-done, bf16[4096,512]{1,0:T(8,128)(2,1)} %all-gather.5.cloned.1.call-done), kind=kOutput, calls=%fused_computation.13 | convolution fusion | flops 2318204928 | bytes 12386304 | tf_op jit(solution)/shard_map/dot_general | solution.py:64
  113.8 0.0 copy-start
  113.8 0.0 copy-start.2
  113.8 0.0 copy-start.3
  113.8 0.0 copy-start.4
  113.8 0.0 copy-start.5
  113.9 0.0 reduce-scatter.2.cloned.1.call-update
  113.9 0.0 all-reduce.2.cloned.1.call-start
  114.0 0.8 copy-done
  114.8 0.7 broadcast_select_fusion
  115.5 0.0 all-reduce.2.cloned.1.call-update
  115.5 229.2 %reduce-scatter.2.cloned.1.call-done = f32[16,1792]{1,0:T(8,128)} async-done(((f32[512,1792]{1,0:T(8,128)}), f32[16,1792]{1,0:T(8,128)}) %reduce-scatter.2.cloned.1.call-update) | async-done | bytes 114704 | tf_op jit(solution)/shard_map/reduce_scatter | solution.py:63
  344.8 0.0 copy-done.2
  344.8 0.0 copy-done.3
  344.8 0.0 copy-done.4
  344.8 0.0 copy-done.5
  344.8 1.6 divide_convert_fusion
  346.4 81.5 %all_gather.14 = bf16[512,896]{1,0:T(8,128)(2,1)S(1)} all-gather(bf16[16,896]{1,0:T(8,128)(2,1)S(1)} %get-tuple-element.14), channel_id=1, replica_groups=mesh['dp'=32,'fsdp'=16] {'dp'}, dimensions={0}, use_global_device_ids=true | all-gather | bytes 946176 | tf_op jit(solution)/shard_map/all_gather | solution.py:75
  427.8 86.6 %all_gather.15 = bf16[512,896]{1,0:T(8,128)(2,1)S(1)} all-gather(bf16[16,896]{1,0:T(8,128)(2,1)S(1)} %get-tuple-element.6), channel_id=1, replica_groups=mesh['dp'=32,'fsdp'=16] {'dp'}, dimensions={0}, use_global_device_ids=true | all-gather | bytes 946176 | tf_op jit(solution)/shard_map/all_gather | solution.py:76
  514.4 0.0 all-reduce.2.cloned.1.call-done
  514.4 0.0 copy-start.1
  514.4 2.1 fusion.14
  516.5 0.0 copy-done.1
  516.5 1.1 fusion.12
Async XLA Ops:
  7.2 53.8 %all-gather.3.cloned.1.call-start = ((), (), s32[]{:S(2)}) async-start(), calls=%async_computation.2 | async-start | bytes 3342336 | tf_op jit(solution)/shard_map/all_gather | solution.py:46
  7.9 98.1 %all-gather.5.cloned.1.call-start = ((), (), s32[]{:S(2)}) async-start(), calls=%async_computation.3 | async-start | bytes 4456448 | tf_op jit(solution)/shard_map/all_gather | solution.py:49
  8.7 336.1 %reduce-scatter.2.cloned.1.call-start = ((), (), s32[]{:S(2)}) async-start(), calls=%async_computation.4 | async-start | bytes 3784704 | tf_op jit(solution)/shard_map/reduce_scatter | solution.py:63
  113.8 0.9 copy-start
  113.8 230.9 %copy-start.2 = (f32[16,896]{1,0:T(8,128)S(1)}, f32[16,896]{1,0:T(8,128)}, u32[]{:S(2)}) copy-start(f32[16,896]{1,0:T(8,128)} %param.17) | copy-start | bytes 172036
  113.8 230.9 %copy-start.3 = (f32[16,896]{1,0:T(8,128)S(1)}, f32[16,896]{1,0:T(8,128)}, u32[]{:S(2)}) copy-start(f32[16,896]{1,0:T(8,128)} %param.16) | copy-start | bytes 172036
  113.8 230.9 %copy-start.4 = (f32[16,896]{1,0:T(8,128)S(1)}, f32[16,896]{1,0:T(8,128)}, u32[]{:S(2)}) copy-start(f32[16,896]{1,0:T(8,128)} %param.15) | copy-start | bytes 172036
  113.8 230.9 %copy-start.5 = (f32[16,896]{1,0:T(8,128)S(1)}, f32[16,896]{1,0:T(8,128)}, u32[]{:S(2)}) copy-start(f32[16,896]{1,0:T(8,128)} %param.14) | copy-start | bytes 172036
  113.9 400.6 %all-reduce.2.cloned.1.call-start = ((), (), s32[]{:S(2)}) async-start(), calls=%async_computation.1 | async-start | bytes 524288 | tf_op jit(solution)/shard_map/psum | solution.py:9
  514.4 2.1 copy-start.1
Sparse Core Ops, SparseCore 0:
  10.1 50.8 all-gather.2
  63.1 42.8 all-gather.4
  114.0 230.7 reduce-scatter.1
  348.4 124.2 all-reduce.1
where the time goes:
time: 524 us
  waiting for transfers between devices  326 us (62%)
  blocking collectives  168 us (32%)
  between operations  13.8 us (3%)
  matrix products  11 us (2%)
    reduce_scatter x1, waiting for transfers between devices, per_device(): lax.psum_scatter(lax.dot_general(projected, both, (((0,), (0,)), ((), ())...  229 us
    all_gather x1, blocking collectives, per_device(): lax.all_gather(linear_norm, 'dp', axis=0, tiled=True)  86.6 us
    all_gather x1, blocking collectives, per_device(): lax.all_gather(gate_norm, 'dp', axis=0, tiled=True)  81.5 us
    all_gather x1, waiting for transfers between devices, per_device(): features = lax.all_gather(tokens, 'fsdp', axis=1, tiled=True)  50 us
    all_gather x1, waiting for transfers between devices, per_device(): lax.all_gather(basis, 'fsdp', axis=0, tiled=True)  45 us
  transfers between devices with their start and end apart: 4, of which 3 were waited for; matrix products, arithmetic and copies ran while one was open for 1% of the time, Pallas kernels for 0%

commit v1 on v0

--- a/solution.py
+++ b/solution.py
@@ -72,7 +72,11 @@
     moment_linear, second_linear, linear_norm = adam_step(
         linear_moment, linear_second, subspace[:, width:]
     )
-    gate_update = expand_one(lax.all_gather(gate_norm, "dp", axis=0, tiled=True))
+    gate_update = expand_one(
+        jnp.concatenate(
+            lax.all_to_all(jnp.stack([gate_norm] * lax.axis_size("dp")), "dp", 0, 0), axis=0
+        )
+    )
     linear_update = expand_one(lax.all_gather(linear_norm, "dp", axis=0, tiled=True))
     return (gate_update, linear_update, moment_gate, second_gate, moment_linear, second_linear)
 

time: 524 us -> 499 us (0.952)
  the two profiles are of different devices: /device:TPU:16 before, /device:TPU:1 now
where the time goes in v1:
time: 499 us
  waiting for transfers between devices  380 us (76%)
  blocking collectives  81 us (16%)
  between operations  13.8 us (3%)
  matrix products  10.9 us (2%)
  starting transfers between devices  7.25 us (1%)
    reduce_scatter x1, waiting for transfers between devices, per_device(): lax.psum_scatter(lax.dot_general(projected, both, (((0,), (0,)), ((), ())...  226 us
    all_gather x1, blocking collectives, per_device(): lax.all_gather(linear_norm, 'dp', axis=0, tiled=True)  81 us
    psum x1, waiting for transfers between devices, spread(): return lax.psum(kept, axis)  55.9 us
    all_gather x1, waiting for transfers between devices, per_device(): features = lax.all_gather(tokens, 'fsdp', axis=1, tiled=True)  52.1 us
    all_gather x1, waiting for transfers between devices, per_device(): lax.all_gather(basis, 'fsdp', axis=0, tiled=True)  44.3 us
  transfers between devices with their start and end apart: 5, of which 4 were waited for; matrix products, arithmetic and copies ran while one was open for 1% of the time, Pallas kernels for 0%

profile of v1, /device:TPU:1, one launch (start us, length us, event | category | flops | bytes accessed | tf_op | source)
XLA Modules:
  0.0 498.8 jit_solution(8979243173092363294)
XLA Ops:
  7.2 0.0 all-gather.3.cloned.1.call-start
  7.2 0.7 all-gather.3.cloned.1.call-update
  7.9 0.0 all-gather.5.cloned.1.call-start
  7.9 0.7 all-gather.5.cloned.1.call-update
  8.7 0.0 reduce-scatter.2.cloned.1.call-start
  8.7 2.3 fusion.2
  11.0 52.1 %all-gather.3.cloned.1.call-done = bf16[384,4096]{1,0:T(8,128)(2,1)} async-done(((bf16[384,256]{1,0:T(8,128)(2,1)}), bf16[384,4096]{1,0:T(8,128)(2,1)}) %all-gather.3.cloned.1.call-update) | async-done | bytes 3145744 | tf_op jit(solution)/shard_map/all_gather | solution.py:46
  63.1 44.3 %all-gather.5.cloned.1.call-done = bf16[4096,512]{1,0:T(8,128)(2,1)} async-done(((bf16[256,512]{1,0:T(8,128)(2,1)}), bf16[4096,512]{1,0:T(8,128)(2,1)}) %all-gather.5.cloned.1.call-update) | async-done | bytes 4194320 | tf_op jit(solution)/shard_map/all_gather | solution.py:49
  107.4 7.8 %fusion.8 = f32[512,1792]{1,0:T(8,128)} fusion(bf16[384,896]{1,0:T(8,128)(2,1)S(1)} %get-tuple-element.13, bf16[384,896]{1,0:T(8,128)(2,1)S(1)} %get-tuple-element.12, bf16[384,4096]{1,0:T(8,128)(2,1)} %all-gather.3.cloned.1.call-done, bf16[4096,512]{1,0:T(8,128)(2,1)} %all-gather.5.cloned.1.call-done), kind=kOutput, calls=%fused_computation.13 | convolution fusion | flops 2318204928 | bytes 12386304 | tf_op jit(solution)/shard_map/dot_general | solution.py:64
  115.2 0.0 copy-start.2
  115.2 0.0 copy-start.3
  115.2 0.0 copy-start.4
  115.2 0.0 copy-start.5
  115.3 0.0 reduce-scatter.2.cloned.1.call-update
  115.3 226.4 %reduce-scatter.2.cloned.1.call-done = f32[16,1792]{1,0:T(8,128)} async-done(((f32[512,1792]{1,0:T(8,128)}), f32[16,1792]{1,0:T(8,128)}) %reduce-scatter.2.cloned.1.call-update) | async-done | bytes 114704 | tf_op jit(solution)/shard_map/reduce_scatter | solution.py:63
  341.6 0.0 copy-done.2
  341.6 0.0 copy-done.3
  341.6 0.0 copy-done.4
  341.6 0.0 copy-done.5
  341.6 1.6 divide_convert_fusion
  343.2 0.0 copy-start
  343.2 1.0 stack.2
  344.2 7.1 %all-to-all-start = ((bf16[32,16,896]{2,1,0:T(8,128)(2,1)}), bf16[32,16,896]{2,1,0:T(8,128)(2,1)S(1)}, u32[]{:S(2)}, u32[]{:S(2)}) async-start(bf16[32,16,896]{2,1,0:T(8,128)(2,1)} %stack.2), calls=%async_computation.1 | async-start | bytes 1835008 | tf_op jit(solution)/shard_map/all_to_all | solution.py:77
  351.3 0.0 all-reduce.2.cloned.1.call-start
  351.4 0.0 copy-done
  351.4 0.7 broadcast_select_fusion
  352.1 0.0 all-reduce.2.cloned.1.call-update
  352.2 81.0 %all_gather.11 = bf16[512,896]{1,0:T(8,128)(2,1)S(1)} all-gather(bf16[16,896]{1,0:T(8,128)(2,1)S(1)} %get-tuple-element.6), channel_id=1, replica_groups=mesh['dp'=32,'fsdp'=16] {'dp'}, dimensions={0}, use_global_device_ids=true | all-gather | bytes 946176 | tf_op jit(solution)/shard_map/all_gather | solution.py:80
  433.2 55.9 %all-reduce.2.cloned.1.call-done = bf16[256,512]{1,0:T(8,128)(2,1)} async-done(((bf16[256,512]{1,0:T(8,128)(2,1)}), bf16[256,512]{1,0:T(8,128)(2,1)}) %all-reduce.2.cloned.1.call-update) | async-done | bytes 262160 | tf_op jit(solution)/shard_map/psum | solution.py:9
  489.1 0.0 copy-start.1
  489.1 2.1 fusion.12
  491.2 0.0 all-to-all-done
  491.2 0.0 copy-done.1
  491.2 1.1 fusion.14
Async XLA Ops:
  7.2 55.9 %all-gather.3.cloned.1.call-start = ((), (), s32[]{:S(2)}) async-start(), calls=%async_computation.3 | async-start | bytes 3342336 | tf_op jit(solution)/shard_map/all_gather | solution.py:46
  7.9 99.5 %all-gather.5.cloned.1.call-start = ((), (), s32[]{:S(2)}) async-start(), calls=%async_computation.4 | async-start | bytes 4456448 | tf_op jit(solution)/shard_map/all_gather | solution.py:49
  8.7 333.0 %reduce-scatter.2.cloned.1.call-start = ((), (), s32[]{:S(2)}) async-start(), calls=%async_computation.5 | async-start | bytes 3784704 | tf_op jit(solution)/shard_map/reduce_scatter | solution.py:63
  115.2 226.4 %copy-start.2 = (f32[16,896]{1,0:T(8,128)S(1)}, f32[16,896]{1,0:T(8,128)}, u32[]{:S(2)}) copy-start(f32[16,896]{1,0:T(8,128)} %param.17) | copy-start | bytes 172036
  115.2 226.4 %copy-start.3 = (f32[16,896]{1,0:T(8,128)S(1)}, f32[16,896]{1,0:T(8,128)}, u32[]{:S(2)}) copy-start(f32[16,896]{1,0:T(8,128)} %param.16) | copy-start | bytes 172036
  115.2 226.4 %copy-start.4 = (f32[16,896]{1,0:T(8,128)S(1)}, f32[16,896]{1,0:T(8,128)}, u32[]{:S(2)}) copy-start(f32[16,896]{1,0:T(8,128)} %param.15) | copy-start | bytes 172036
  115.2 226.4 %copy-start.5 = (f32[16,896]{1,0:T(8,128)S(1)}, f32[16,896]{1,0:T(8,128)}, u32[]{:S(2)}) copy-start(f32[16,896]{1,0:T(8,128)} %param.14) | copy-start | bytes 172036
  343.2 8.2 %copy-start = (bf16[256,512]{1,0:T(8,128)(2,1)S(1)}, bf16[256,512]{1,0:T(8,128)(2,1)}, u32[]{:S(2)}) copy-start(bf16[256,512]{1,0:T(8,128)(2,1)} %param.13) | copy-start | bytes 786436
  344.2 147.0 %all-to-all-start = ((bf16[32,16,896]{2,1,0:T(8,128)(2,1)}), bf16[32,16,896]{2,1,0:T(8,128)(2,1)S(1)}, u32[]{:S(2)}, u32[]{:S(2)}) async-start(bf16[32,16,896]{2,1,0:T(8,128)(2,1)} %stack.2), calls=%async_computation.1 | async-start | bytes 1835008 | tf_op jit(solution)/shard_map/all_to_all | solution.py:77
  351.3 137.8 %all-reduce.2.cloned.1.call-start = ((), (), s32[]{:S(2)}) async-start(), calls=%async_computation.2 | async-start | bytes 524288 | tf_op jit(solution)/shard_map/psum | solution.py:9
  489.1 2.1 copy-start.1
Sparse Core Ops, SparseCore 0:
  10.1 52.9 all-gather.2
  65.2 42.1 all-gather.4
  115.4 226.1 reduce-scatter.1
  355.6 133.4 all-reduce.1
